TPU v7x, 32 devices: a whole 2x2x4 slice. The times are simulated.
32 devices in a mesh: row: 2 (over y), col: 16 (over z, x, core).
Axes of the slice: x: 2, y: 2, z: 4, core: 2. Of those that a mesh axis runs over, the one named last changes fastest.
Arguments:
- strip: float32 [12, 2048, 2, 1024], P(None, 'col', None, 'row'), may hold values from -6 to 6
- lower: float32 [12, 2048, 2, 1024], P(None, 'col', None, 'row'), may hold values from -1.6 to 1.6, as said below
Outputs:
- reduced: float32 [12, 2048, 2, 1024], P(None, 'col', None, 'row')
Inputs may be any that keep to these rules, and one draw needn't show every extreme that they name: `lower`: in the first 2048 rows the diagonal lies between 0.8 and 1.6 and entries above it are zero.
All inputs are finite; a program needn't handle non-finite values.
Results may differ from a plain program's by a relative error of at most 0.00013.
Values sent between devices are 32-bit elements; how exact they have to be, the bound alone decides.
A program may use at most 128 MiB of HBM per device.

v0:
```python
import jax
import jax.numpy as jnp
from jax import lax
from jax.sharding import PartitionSpec as P

highest = lax.Precision.HIGHEST


def spread(array, axis, root):
    mine = lax.axis_index(axis) == root
    return lax.psum(jnp.where(mine, array, jnp.zeros_like(array)), axis)


def times_rows(coeff, right_side):
    return jnp.dot(coeff, right_side, precision=highest, preferred_element_type=jnp.float32)


def times_rows_turned(coeff, right_turned):
    return lax.dot_general(
        coeff,
        right_turned,
        (((1,), (1,)), ((), ())),
        precision=highest,
        preferred_element_type=jnp.float32,
    )


def local(strip, lower):
    rounds = strip.shape[0]
    strip_width = strip.shape[1]
    row_run = strip.shape[3]
    row_count = lax.axis_size("row")
    block_size = row_run * row_count
    cols_here = rounds * strip_width
    trail_count = cols_here - strip_width
    local_strip = strip.reshape(cols_here, 2, row_run)
    left_part = local_strip[:, 0, :]
    right_part = local_strip[:, 1, :]
    gathered = lax.all_gather(lower[0], "col", axis=0, tiled=True)
    first_cols = gathered[:block_size, 0, :]
    cross_cols = gathered[block_size:, 0, :]
    second_cols = gathered[block_size:, 1, :]
    inverse_all = lax.all_gather(second_cols, "row", axis=1, tiled=True)
    mixed_cols = jnp.dot(
        inverse_all, cross_cols, precision=highest, preferred_element_type=jnp.float32
    )
    upper_half = lax.psum_scatter(
        times_rows_turned(first_cols, left_part), "row", scatter_dimension=0, tiled=True
    )
    carried = lax.psum_scatter(
        times_rows(cross_cols, upper_half), "row", scatter_dimension=0, tiled=True
    )
    remainder = right_part.T - carried
    lower_half = lax.psum_scatter(
        times_rows(second_cols, remainder), "row", scatter_dimension=0, tiled=True
    )
    solved = jnp.stack([upper_half.T, lower_half.T], axis=1)
    lead_rows = solved[:strip_width].reshape(strip_width, 2 * row_run)
    tail_rows = solved[strip_width:].reshape(trail_count, 2 * row_run)
    col_position = lax.axis_index("col")
    offset = col_position * strip_width
    part_block = offset // block_size
    inside = offset % block_size
    root_row = inside // row_run
    shift_in = inside % row_run
    zero_index = jnp.zeros((), jnp.int32)
    mirror_piece = lax.dynamic_slice(
        gathered, (zero_index, part_block, shift_in), (2 * block_size, 1, strip_width)
    )
    mirror_piece = mirror_piece.reshape(2 * block_size, strip_width)
    mirrored = spread(mirror_piece, "row", root_row)
    first_flag = (part_block == 0).astype(jnp.float32)
    second_flag = 1.0 - first_flag
    row_position = lax.axis_index("row")
    first_rows = lax.dynamic_slice_in_dim(mirrored, row_position * row_run, row_run, 0)
    partial_mix = jnp.dot(
        mixed_cols, first_rows, precision=highest, preferred_element_type=jnp.float32
    )
    chained = lax.psum(partial_mix, "row")
    coeff_whole = jnp.concatenate(
        [
            first_flag * mirrored[:block_size],
            second_flag * mirrored[block_size:] - first_flag * chained,
        ],
        axis=0,
    )
    solved_lead = lax.psum_scatter(
        times_rows(coeff_whole, lead_rows), "col", scatter_dimension=0, tiled=True
    )
    everything = lax.all_gather(solved_lead, "col", axis=0, tiled=True)
    left_rows = lower[1:].reshape(trail_count, 2 * row_run)
    grouped = everything.reshape(2, row_count, row_run, 2 * row_run).transpose(1, 0, 2, 3)
    swapped = lax.all_to_all(grouped, "row", split_axis=0, concat_axis=0, tiled=True)
    turned_block = swapped.reshape(row_count, 2, row_run, 2, row_run).transpose(0, 3, 4, 1, 2)
    turned_block = turned_block.reshape(row_count * 2 * row_run, 2 * row_run)
    summed = lax.psum_scatter(
        times_rows_turned(turned_block, left_rows), "row", scatter_dimension=0, tiled=True
    )
    update = summed.T
    reduced = jnp.concatenate([solved_lead, tail_rows - update], axis=0)
    return reduced.reshape(rounds, strip_width, 2, row_run)


def solution(mesh):
    in_specs = (P(None, "col", None, "row"), P(None, "col", None, "row"))
    out_specs = P(None, "col", None, "row")
    return jax.shard_map(local, mesh=mesh, in_specs=in_specs, out_specs=out_specs, check_vma=False)
```

profile of v0, /device:TPU:0, one launch (start us, length us, event | category | flops | bytes accessed | tf_op | source)
XLA Modules:
  0.0 999.0 jit_solution(8596684741201321054)
XLA Ops:
  6.5 0.0 all-gather.8.cloned.1.call-start
  6.5 1.9 slice_bitcast_fusion.3
  8.5 0.0 all-gather.8.cloned.1.call-update
  8.5 0.0 reduce-scatter.6.cloned.1.call-start
  8.5 6.7 copy.12
  15.2 71.9 %all-gather.8.cloned.1.call-done = f32[1,2048,2,512]{3,2,0,1:T(2,128)} async-done(((f32[1,128,2,512]{3,2,0,1:T(2,128)}), f32[1,2048,2,512]{3,2,0,1:T(2,128)}) %all-gather.8.cloned.1.call-update) | async-done | bytes 8388624 | tf_op jit(solution)/shard_map/all_gather | solution.py:39
  87.1 9.5 fusion.23
  96.7 12.2 %fusion.5 = f32[1024,1536]{1,0:T(8,128)} fusion(f32[1536,2,512]{2,0,1:T(8,128)S(1)} %bitcast.69, f32[1024,1,512]{2,1,0:T(1,128)S(1)} %get-tuple-element.7), kind=kOutput, calls=%fused_computation.12 | convolution fusion | flops 9663676416 | bytes 11534336 | tf_op jit(solution)/shard_map/dot_general | solution.py:19
  108.9 0.0 reduce-scatter.6.cloned.1.call-update
  108.9 0.0 all-gather.10.cloned.1.call-start
  109.0 0.7 all-gather.10.cloned.1.call-update
  109.7 0.0 all-reduce.3.cloned.1.call-start
  109.8 3.9 constant_dynamic-slice_fusion
  113.7 1.1 select_bitcast_fusion
  114.8 0.0 all-reduce.3.cloned.1.call-update
  114.8 0.3 reduce-scatter.8.cloned.1.call-start
  115.1 69.4 %reduce-scatter.6.cloned.1.call-done = f32[512,1536]{1,0:T(8,128)} async-done(((f32[1024,1536]{1,0:T(8,128)}), f32[512,1536]{1,0:T(8,128)}) %reduce-scatter.6.cloned.1.call-update) | async-done | bytes 3145744 | tf_op jit(solution)/shard_map/reduce_scatter | solution.py:47
  184.4 0.0 copy-done.3
  184.4 23.0 %convolution_bitcast_fusion.1 = f32[1024,1536]{0,1:T(8,128)} fusion(f32[512,1536]{1,0:T(8,128)} %reduce-scatter.6.cloned.1.call-done, f32[1024,1,512]{2,1,0:T(1,128)S(1)} %get-tuple-element.6), kind=kOutput, calls=%fused_computation.5 | convolution fusion | flops 9663676416 | bytes 11534336 | tf_op jit(solution)/shard_map/dot_general | solution.py:15
  207.4 0.0 reduce-scatter.8.cloned.1.call-update
  207.4 0.4 all-reduce.5.cloned.1.call-start
  207.9 0.0 copy-start.2
  207.9 34.9 %all-gather.10.cloned.1.call-done = f32[1024,1,1024]{2,1,0:T(1,128)} async-done(((f32[1024,1,512]{2,1,0:T(1,128)}), f32[1024,1,1024]{2,1,0:T(1,128)}) %all-gather.10.cloned.1.call-update) | async-done | bytes 4194320 | tf_op jit(solution)/shard_map/all_gather | solution.py:43
  242.8 10.9 %fusion = f32[1024,512]{1,0:T(8,128)} fusion(f32[1024,1,1024]{2,1,0:T(1,128)} %all-gather.10.cloned.1.call-done, f32[1024,1,512]{2,1,0:T(1,128)} %copy-done.3), kind=kOutput, calls=%fused_computation.6 | convolution fusion | flops 6442450944 | bytes 8388608 | tf_op jit(solution)/shard_map/dot_general | solution.py:44
  253.6 31.5 %all-reduce.3.cloned.1.call-done = f32[2048,128]{1,0:T(8,128)} async-done(((f32[2048,128]{1,0:T(8,128)}), f32[2048,128]{1,0:T(8,128)}) %all-reduce.3.cloned.1.call-update) | async-done | bytes 1048592 | tf_op jit(solution)/shard_map/psum | solution.py:11
  285.1 4.2 fusion.19
  289.3 0.0 all-reduce.5.cloned.1.call-update
  289.3 0.0 reduce-scatter.10.cloned.1.call-start
  289.4 75.0 %reduce-scatter.8.cloned.1.call-done = f32[512,1536]{0,1:T(8,128)} async-done(((f32[1024,1536]{0,1:T(8,128)}), f32[512,1536]{0,1:T(8,128)}) %reduce-scatter.8.cloned.1.call-update) | async-done | bytes 3145744 | tf_op jit(solution)/shard_map/reduce_scatter | solution.py:50
  364.3 0.0 copy-done.2
  364.3 13.6 %convolution_bitcast_fusion = f32[1024,1536]{1,0:T(8,128)} fusion(f32[512,1536]{0,1:T(8,128)} %reduce-scatter.8.cloned.1.call-done, f32[1536,2,512]{2,0,1:T(8,128)} %bitcast.68, f32[1024,1,512]{2,1,0:T(1,128)S(1)} %copy-done.2), kind=kOutput, calls=%fused_computation.4 | convolution fusion | flops 9664462848 | bytes 14680064 | tf_op jit(solution)/shard_map/dot_general | solution.py:15
  377.9 0.0 reduce-scatter.10.cloned.1.call-update
  377.9 0.2 reduce-scatter.12.cloned.1.call-start
  378.2 17.1 %all-reduce.5.cloned.1.call-done = f32[1024,128]{1,0:T(8,128)} async-done(((f32[1024,128]{1,0:T(8,128)}), f32[1024,128]{1,0:T(8,128)}) %all-reduce.5.cloned.1.call-update) | async-done | bytes 524304 | tf_op jit(solution)/shard_map/psum | solution.py:79
  395.2 2.4 slice_multiply_fusion.1
  397.6 77.0 %reduce-scatter.10.cloned.1.call-done = f32[512,1536]{1,0:T(8,128)} async-done(((f32[1024,1536]{1,0:T(8,128)}), f32[512,1536]{1,0:T(8,128)}) %reduce-scatter.10.cloned.1.call-update) | async-done | bytes 3145744 | tf_op jit(solution)/shard_map/reduce_scatter | solution.py:54
  474.6 0.0 copy-done
  474.6 1.1 pad_maximum_fusion.2
  475.7 0.0 copy-done.5
  475.7 0.2 copy-done.6
  475.9 8.9 fusion.14
  484.8 0.0 reduce-scatter.12.cloned.1.call-update
  484.8 0.0 all-gather.6.cloned.1.call-start
  484.9 104.8 %reduce-scatter.12.cloned.1.call-done = f32[128,1024]{1,0:T(8,128)} async-done(((f32[2048,1024]{1,0:T(8,128)}), f32[128,1024]{1,0:T(8,128)}) %reduce-scatter.12.cloned.1.call-update) | async-done | bytes 524304 | tf_op jit(solution)/shard_map/reduce_scatter | solution.py:87
  589.7 0.0 all-gather.6.cloned.1.call-update
  589.7 77.1 %all-gather.6.cloned.1.call-done = f32[2048,1024]{1,0:T(8,128)} async-done(((f32[128,1024]{1,0:T(8,128)}), f32[2048,1024]{1,0:T(8,128)}) %all-gather.6.cloned.1.call-update) | async-done | bytes 8388624 | tf_op jit(solution)/shard_map/all_gather | solution.py:90
  666.7 8.3 copy.49
  675.0 6.9 all-to-all-start
  681.9 0.0 reduce-scatter.14.cloned.1.call-start
  682.0 0.0 slice-start
  682.0 2.6 slice-done
  684.6 3.9 copy.27
  688.6 86.4 %all-to-all-done = f32[2,2,512,1024]{3,2,1,0:T(8,128)} async-done(((f32[2,2,512,1024]{3,2,1,0:T(8,128)}), f32[2,2,512,1024]{3,2,1,0:T(8,128)}, u32[]{:S(2)}, u32[]{:S(2)}) %all-to-all-start) | async-done | bytes 8388640 | tf_op jit(solution)/shard_map/all_to_all | solution.py:93
  775.0 13.2 %copy.19 = f32[2,2,512,1024]{2,1,3,0:T(2,128)} copy(f32[2,2,512,1024]{3,2,1,0:T(8,128)} %all-to-all-done) | data formatting | bytes 16777216 | tf_op jit(solution)/shard_map/reshape | solution.py:94
  788.2 5.7 copy.26
  793.8 42.9 %fusion.24 = f32[2048,1408]{1,0:T(8,128)} fusion(f32[2048,1024]{1,0:T(8,128)S(1)} %bitcast.74, f32[1408,1024]{1,0:T(8,128)S(1)} %bitcast.76), kind=kOutput, calls=%fused_computation.37 | convolution fusion | flops 35433480192 | bytes 25690112 | tf_op jit(solution)/shard_map/dot_general | solution.py:19
  836.8 0.0 reduce-scatter.14.cloned.1.call-update
  836.8 5.1 pad_maximum_fusion.1
  841.9 1.2 copy.16
  843.1 124.4 %reduce-scatter.14.cloned.1.call-done = f32[1024,1408]{1,0:T(8,128)} async-done(((f32[2048,1408]{1,0:T(8,128)}), f32[1024,1408]{1,0:T(8,128)}) %reduce-scatter.14.cloned.1.call-update) | async-done | bytes 5767184 | tf_op jit(solution)/shard_map/reduce_scatter | solution.py:96
  967.5 4.9 bitcast_subtract_fusion
  972.4 3.6 pad_maximum_fusion
  976.0 6.6 copy.17
  982.6 9.1 reshape.35
  (8 shorter events, 0.0 us)
Async XLA Ops:
  6.5 80.6 %all-gather.8.cloned.1.call-start = ((), (), s32[]{:S(2)}) async-start(), calls=%async_computation.14 | async-start | bytes 8912896 | tf_op jit(solution)/shard_map/all_gather | solution.py:39
  8.5 175.9 %reduce-scatter.6.cloned.1.call-start = ((), (), s32[]{:S(2)}) async-start(), calls=%async_computation.8 | async-start | bytes 9437184 | tf_op jit(solution)/shard_map/reduce_scatter | solution.py:47
  87.1 9.6 copy-start.1
  96.7 87.7 %copy-start.3 = (f32[1024,1,512]{2,1,0:T(1,128)}, f32[1024,1,512]{2,1,0:T(1,128)S(1)}, u32[]{:S(2)}) copy-start(f32[1024,1,512]{2,1,0:T(1,128)S(1)} %get-tuple-element.6) | copy-start | bytes 6291460
  108.9 133.8 %all-gather.10.cloned.1.call-start = ((), (), s32[]{:S(2)}) async-start(), calls=%async_computation.15 | async-start | bytes 6291456 | tf_op jit(solution)/shard_map/all_gather | solution.py:43
  109.7 175.4 %all-reduce.3.cloned.1.call-start = ((), (), s32[]{:S(2)}) async-start(), calls=%async_computation.6 | async-start | bytes 2097152 | tf_op jit(solution)/shard_map/psum | solution.py:11
  114.8 249.5 %reduce-scatter.8.cloned.1.call-start = ((), (), s32[]{:S(2)}) async-start(), calls=%async_computation.9 | async-start | bytes 9437184 | tf_op jit(solution)/shard_map/reduce_scatter | solution.py:50
  207.4 187.8 %all-reduce.5.cloned.1.call-start = ((), (), s32[]{:S(2)}) async-start(), calls=%async_computation.7 | async-start | bytes 1048576 | tf_op jit(solution)/shard_map/psum | solution.py:79
  207.9 156.5 %copy-start.2 = (f32[1024,1,512]{2,1,0:T(1,128)S(1)}, f32[1024,1,512]{2,1,0:T(1,128)}, u32[]{:S(2)}) copy-start(f32[1024,1,512]{2,1,0:T(1,128)} %get-tuple-element.5) | copy-start | bytes 6291460
  289.3 185.3 %reduce-scatter.10.cloned.1.call-start = ((), (), s32[]{:S(2)}) async-start(), calls=%async_computation.10 | async-start | bytes 9437184 | tf_op jit(solution)/shard_map/reduce_scatter | solution.py:54
  377.9 96.7 %copy-start = (f32[512,1536]{1,0:T(8,128)S(1)}, f32[512,1536]{1,0:T(8,128)}, u32[]{:S(2)}) copy-start(f32[512,1536]{1,0:T(8,128)} %reduce-scatter.6.cloned.1.call-done) | copy-start | bytes 9437188
  377.9 211.7 %reduce-scatter.12.cloned.1.call-start = ((), (), s32[]{:S(2)}) async-start(), calls=%async_computation.11 | async-start | bytes 8912896 | tf_op jit(solution)/shard_map/reduce_scatter | solution.py:87
  474.6 1.1 copy-start.5
  474.6 1.3 copy-start.6
  484.8 181.9 %all-gather.6.cloned.1.call-start = ((), (), s32[]{:S(2)}) async-start(), calls=%async_computation.12 | async-start | bytes 8912896 | tf_op jit(solution)/shard_map/all_gather | solution.py:90
  675.0 100.0 %all-to-all-start = ((f32[2,2,512,1024]{3,2,1,0:T(8,128)}), f32[2,2,512,1024]{3,2,1,0:T(8,128)}, u32[]{:S(2)}, u32[]{:S(2)}) async-start(f32[2,2,512,1024]{3,2,1,0:T(8,128)} %bitcast.66), calls=%async_computation.4 | async-start | bytes 16777216 | tf_op jit(solution)/shard_map/all_to_all | solution.py:93
  681.9 285.6 %reduce-scatter.14.cloned.1.call-start = ((), (), s32[]{:S(2)}) async-start(), calls=%async_computation.13 | async-start | bytes 17301504 | tf_op jit(solution)/shard_map/reduce_scatter | solution.py:96
  682.0 2.6 slice-start
  788.2 5.7 copy-start.4
Sparse Core Ops, SparseCore 0:
  9.5 77.5 all-gather.7
  109.1 75.3 reduce-scatter.5
  186.0 56.6 all-gather.9
  245.0 40.0 all-reduce.2
  287.2 77.0 reduce-scatter.7
  366.6 28.5 all-reduce.4
  397.5 77.0 reduce-scatter.9
  484.9 104.6 reduce-scatter.11
  592.0 74.6 all-gather.5
  836.9 130.5 reduce-scatter.13
where the time goes:
time: 1010 us; the launch traced here: 999 us
  waiting for transfers between devices  770 us (76%)
  matrix products  116 us (11%)
  local copies, waits for them, and re-layouts  72.9 us (7%)
  other arithmetic  18.1 us (2%)
  between operations  14.1 us (1%)
    reduce_scatter x1, waiting for transfers between devices, local(): lax.psum_scatter(times_rows_turned(turned_block, left_rows), 'row', scatt...  124 us
    reduce_scatter x1, waiting for transfers between devices, local(): lax.psum_scatter(times_rows(coeff_whole, lead_rows), 'col', scatter_dimen...  105 us
    all_to_all x1, waiting for transfers between devices, local(): lax.all_to_all(grouped, 'row', split_axis=0, concat_axis=0, tiled=True)  86.4 us
    all_gather x1, waiting for transfers between devices, local(): everything = lax.all_gather(solved_lead, 'col', axis=0, tiled=True)  77.1 us
    reduce_scatter x1, waiting for transfers between devices, local(): lax.psum_scatter(times_rows(second_cols, remainder), 'row', scatter_dimen...  77 us
    reduce_scatter x1, waiting for transfers between devices, local(): lax.psum_scatter(times_rows(cross_cols, upper_half), 'row', scatter_dimen...  75 us
    all_gather x1, waiting for transfers between devices, local(): gathered = lax.all_gather(lower[0], 'col', axis=0, tiled=True)  71.9 us
    reduce_scatter x1, waiting for transfers between devices, local(): lax.psum_scatter(times_rows_turned(first_cols, left_part), 'row', scatter...  69.4 us
  transfers between devices with their start and end apart: 11, of which 11 were waited for; matrix products, arithmetic and copies ran while one was open for 8% of the time, Pallas kernels for 0%

commit v1 on v0

v1 whole, which is shorter than its diff:
```python
import jax
import jax.numpy as jnp
from jax import lax
from jax.sharding import PartitionSpec as P

PREC = lax.Precision.HIGH


def mm(a, b):
    return jnp.dot(a, b, precision=PREC, preferred_element_type=jnp.float32)


def mm_t(a, b):
    return lax.dot_general(
        a, b, (((1,), (1,)), ((), ())), precision=PREC, preferred_element_type=jnp.float32
    )


def row_parts(x):
    n = lax.axis_size("row")
    parts = [x]
    for s in range(1, n):
        parts.append(lax.ppermute(x, "row", [((i + s) % n, i) for i in range(n)]))
    return parts


def in_order(parts, r):
    n = len(parts)
    twice = jnp.stack(parts + parts[:-1], axis=0)
    return lax.dynamic_slice_in_dim(twice, (n - r) % n, n, 0)


def local(strip, lower):
    rounds, width, _, run = strip.shape
    n_row = lax.axis_size("row")
    n_col = lax.axis_size("col")
    block = run * n_row
    r = lax.axis_index("row")
    c = lax.axis_index("col")
    half = n_col // 2
    tail = (rounds - 1) * width

    lead_l = lower[0]
    first = lax.all_gather(lead_l[:, 0, :], ("col", "row"), axis=0)
    first = first.reshape(n_col, n_row, width, run).transpose(0, 2, 1, 3).reshape(2 * block, block)
    e0, f = first[:block], first[block:]
    e1_mine = lead_l[:, 1, :]
    cut = width // 2
    moved = lax.ppermute(e1_mine[:cut], "col", [(half + i, i) for i in range(half)])
    e1_share = jnp.where(c < half, moved, e1_mine[cut:])
    second = lax.all_gather(e1_share, ("col", "row"), axis=0)
    second = second.reshape(2, half, n_row, cut, run).transpose(1, 0, 3, 2, 4)
    e1 = second.reshape(block, block)

    lead_s = in_order(row_parts(strip[0]), r)
    s0 = lead_s[:, :, 0, :].transpose(1, 0, 2).reshape(width, block)
    s1 = lead_s[:, :, 1, :].transpose(1, 0, 2).reshape(width, block)

    s_parts = row_parts(strip[1:])
    g_parts = row_parts(lower[1:])

    e0_rows = lax.dynamic_slice_in_dim(e0, r * run, run, 0)
    e1_rows = lax.dynamic_slice_in_dim(e1, r * run, run, 0)

    y0 = mm_t(e0, s0)
    r1 = s1.T - mm(f, y0)
    y1 = mm(e1_rows, r1)
    y = jnp.concatenate([lax.dynamic_slice_in_dim(y0, r * run, run, 0), y1], axis=0)
    share = 2 * run // n_col
    zt = lax.all_to_all(y.reshape(n_col, share, width), "col", split_axis=0, concat_axis=0, tiled=True)
    zt = zt.transpose(1, 0, 2).reshape(share, 2 * block)
    c0 = mm_t(zt[:, :block], e0)
    c1 = mm_t(zt[:, block:] - mm_t(c0, f), e1)
    ct = lax.all_gather(jnp.concatenate([c0, c1], axis=1), "col", axis=0, tiled=True)

    x_rows = mm(mm(e1_rows, f), e0)

    def columns(m, s):
        return lax.dynamic_slice_in_dim(m, lax.rem(r + s, n_row) * run, run, 1)

    z0 = 0.0
    z1 = 0.0
    for s, part in enumerate(s_parts):
        part = part.reshape(tail, 2, run)
        z0 = z0 + mm_t(part[:, 0, :], columns(e0_rows, s))
        z1 = z1 + mm_t(part[:, 1, :], columns(e1_rows, s)) - mm_t(part[:, 0, :], columns(x_rows, s))
    out = jnp.concatenate([z0, z1], axis=1)
    for s, part in enumerate(g_parts):
        part = part.reshape(tail, 2, run)
        out = out - mm_t(part[:, 0, :], columns(ct[:, :block], s))
        out = out - mm_t(part[:, 1, :], columns(ct[:, block:], s))
    lead = lax.dynamic_slice_in_dim(ct, c * width, width, 1).T
    reduced = jnp.concatenate([lead, out], axis=0)
    return reduced.reshape(rounds, width, 2, run)


def solution(mesh):
    spec = P(None, "col", None, "row")
    return jax.shard_map(local, mesh=mesh, in_specs=(spec, spec), out_specs=spec, check_vma=False)
```

time: 1010 us -> 596 us (0.59)
  waiting for transfers between devices: 770 us -> 353 us
  matrix products: 116 us -> 78 us
  local copies, waits for them, and re-layouts: 72.9 us -> 109 us
  blocking collectives: 0 us -> 18.4 us
  other arithmetic: 18.1 us -> 7.57 us
    reduce_scatter x5 -> x0, waiting for transfers between devices: 450 us -> none  [the longest x1 124 us: local(): lax.psum_scatter(times_rows_turned(turned_block, left_rows), 'row', scatt...]
    ppermute x0 -> x4, waiting for transfers between devices: none -> 237 us  [the longest x3 227 us: row_parts(): parts.append(lax.ppermute(x, 'row', [((i + s) % n, i) for i in range(n)]))]
    all_to_all x1 -> x0, waiting for transfers between devices: 86.4 us -> none  [local(): lax.all_to_all(grouped, 'row', split_axis=0, concat_axis=0, tiled=True)]
    all_gather x3, waiting for transfers between devices: 184 us -> 115 us  [the longest x1 70.6 us: local(): first = lax.all_gather(lead_l[:, 0, :], ('col', 'row'), axis=0)]
    psum x2 -> x0, waiting for transfers between devices: 48.5 us -> none  [the longest x1 31.5 us: spread(): return lax.psum(jnp.where(mine, array, jnp.zeros_like(array)), axis)]
    slice x3 -> x12, local copies, waits for them, and re-layouts: 12.2 us -> 60.6 us  [the longest x2 18.2 us: local(): z0 = z0 + mm_t(part[:, 0, :], columns(e0_rows, s))]
    dot_general x7 -> x18, matrix products: 116 us -> 78 us  [the longest x14 67.2 us: mm_t(): lax.dot_general(a, b, (((1,), (1,)), ((), ())), precision=PREC, preferred...]
    all_to_all x0 -> x1, blocking collectives: none -> 18.4 us  [local(): lax.all_to_all(y.reshape(n_col, share, width), 'col', split_axis=0, conca...]
  transfers between devices with their start and end apart: 11 -> 7, of which waited for: 11 -> 6; matrix products, arithmetic and copies ran while one was open for 8% -> 16% of each run, Pallas kernels for 0% -> 0%
where the time goes in v1:
time: 596 us; the launch traced here: 586 us
  waiting for transfers between devices  353 us (59%)
  local copies, waits for them, and re-layouts  109 us (18%)
  matrix products  78 us (13%)
  blocking collectives  18.4 us (3%)
  between operations  13.8 us (2%)
  other arithmetic  7.57 us (1%)
    ppermute x3, waiting for transfers between devices, row_parts(): parts.append(lax.ppermute(x, 'row', [((i + s) % n, i) for i in range(n)]))  227 us
    all_gather x1, waiting for transfers between devices, local(): first = lax.all_gather(lead_l[:, 0, :], ('col', 'row'), axis=0)  70.6 us
    dot_general x14, matrix products, mm_t(): lax.dot_general(a, b, (((1,), (1,)), ((), ())), precision=PREC, preferred...  67.2 us
    all_gather x1, waiting for transfers between devices, local(): second = lax.all_gather(e1_share, ('col', 'row'), axis=0)  44.8 us
    all_to_all x1, blocking collectives, local(): lax.all_to_all(y.reshape(n_col, share, width), 'col', split_axis=0, conca...  18.4 us
    slice x2, local copies, waits for them, and re-layouts, local(): z0 = z0 + mm_t(part[:, 0, :], columns(e0_rows, s))  18.2 us
    slice x2, local copies, waits for them, and re-layouts, local(): out = out - mm_t(part[:, 1, :], columns(ct[:, block:], s))  15.1 us
    unnamed x34, local copies, waits for them, and re-layouts  13.8 us
  transfers between devices with their start and end apart: 7, of which 6 were waited for; matrix products, arithmetic and copies ran while one was open for 16% of the time, Pallas kernels for 0%

profile of v1, /device:TPU:0, one launch (start us, length us, event | category | flops | bytes accessed | tf_op | source)
XLA Modules:
  0.0 585.5 jit_solution(15360826118744507567)
XLA Ops:
  6.5 1.1 slice_bitcast_fusion.2
  7.7 0.3 fusion.78
  8.0 1.3 collective-permute-start.1
  9.3 10.3 %collective-permute-done.1 = f32[64,512]{1,0:T(8,128)S(1)} collective-permute-done((f32[64,512]{1,0:T(8,128)S(1)}, f32[64,512]{1,0:T(8,128)S(1)}, u32[]{:S(2)}, u32[]{:S(2)}) %collective-permute-start.1) | collective-permute-done | bytes 131104 | tf_op jit(solution)/shard_map/ppermute | solution.py:49
  19.6 0.7 bitcast_select_fusion
  20.3 0.0 all-gather.8.cloned.1.call-start
  20.3 0.9 slice.116
  21.2 0.0 all-gather.6.cloned.1.call-start
  21.3 0.1 copy.113
  21.4 2.3 collective-permute-start
  23.7 12.0 %collective-permute-done = f32[128,2,512]{2,0,1:T(8,128)S(1)} collective-permute-done((f32[128,2,512]{2,0,1:T(8,128)S(1)}, f32[128,2,512]{2,0,1:T(8,128)S(1)}, u32[]{:S(2)}, u32[]{:S(2)}) %collective-permute-start) | collective-permute-done | bytes 524320 | tf_op jit(solution)/shard_map/ppermute | solution.py:23
  35.7 0.2 fusion.53
  35.9 0.1 slice_bitcast_fusion.1
  36.0 0.2 copy.23
  36.2 0.2 copy.24
  36.4 0.2 copy.19
  36.6 44.8 %all-gather.10.cloned.1.call-done = f32[2048,512]{1,0:T(8,128)} async-done(((f32[64,512]{1,0:T(8,128)}), f32[2048,512]{1,0:T(8,128)}) %all-gather.10.cloned.1.call-update) | async-done | bytes 4194320 | tf_op jit(solution)/shard_map/all_gather | solution.py:51
  81.4 5.4 copy.22
  86.8 3.1 copy.44
  89.9 70.6 %all-gather.8.cloned.1.call-done = f32[4096,1,512]{2,1,0:T(1,128)} async-done(((f32[128,1,512]{2,1,0:T(1,128)}), f32[4096,1,512]{2,1,0:T(1,128)}) %all-gather.8.cloned.1.call-update) | async-done | bytes 8388624 | tf_op jit(solution)/shard_map/all_gather | solution.py:44
  160.5 7.6 %copy.30 = f32[4096,1,512]{2,0,1:T(8,128)} copy(f32[4096,1,512]{2,1,0:T(1,128)} %all-gather.8.cloned.1.call-done) | data formatting | bytes 16777216
  168.1 10.5 %copy.20 = f32[16,2,128,512]{2,0,3,1:T(8,128)} copy(f32[16,2,128,512]{3,2,1,0:T(8,128)} %bitcast.130) | data formatting | bytes 16777216 | tf_op jit(solution)/shard_map/reshape | solution.py:45
  178.6 4.0 fusion.73
  182.6 1.8 fusion.71
  184.5 0.2 copy-done
  184.7 1.3 copy-done.2
  185.9 1.9 fusion.46
  187.8 0.3 copy-done.5
  188.1 1.2 fusion.44
  189.4 0.2 copy.26
  189.5 18.4 %all_to_all.5 = f32[16,64,128]{2,1,0:T(8,128)S(1)} all-to-all(f32[16,64,128]{2,1,0:T(8,128)S(1)} %bitcast.140), channel_id=1, replica_groups=mesh['row'=2,'col'=16] {'col'}, dimensions={0} | all-to-all | bytes 1048576 | tf_op jit(solution)/shard_map/all_to_all | solution.py:70
  208.0 4.2 fusion.60
  212.2 1.9 fusion.49
  214.1 0.3 copy-done.6
  214.4 2.2 fusion.79
  216.6 0.8 pad_maximum_fusion.2
  217.4 7.4 %slice.103 = f32[11,128,2,512]{3,2,1,0:T(2,128)} slice(f32[12,128,2,512]{3,2,1,0:T(2,128)} %param.2), slice={[1:12], [0:128], [0:2], [0:512]} | slice | bytes 11534336 | tf_op jit(solution)/shard_map/slice | solution.py:59
  224.8 0.6 collective-permute-start.2
  225.4 4.5 slice.109
  229.9 1.4 collective-permute-start.3
  231.3 9.1 %fusion.77 = (f32[1408,1,512]{2,1,0:T(1,128)S(1)}, f32[1408,1,512]{2,1,0:T(1,128)S(1)}) fusion(f32[1408,2,512]{2,1,0:T(2,128)} %bitcast.18), kind=kLoop, calls=%fused_computation.94 | loop fusion | bytes 11534336 | tf_op jit(solution)/shard_map/slice | solution.py:85
  240.4 10.4 %fusion.75 = (f32[1408,1,512]{2,1,0:T(1,128)}, f32[1408,1,512]{2,1,0:T(1,128)}) fusion(f32[1408,2,512]{2,1,0:T(2,128)} %bitcast.22), kind=kLoop, calls=%fused_computation.92 | loop fusion | bytes 11534336 | tf_op jit(solution)/shard_map/slice | solution.py:90
  250.8 101.4 %collective-permute-done.2 = f32[11,128,2,512]{3,2,1,0:T(2,128)} collective-permute-done((f32[11,128,2,512]{3,2,1,0:T(2,128)}, f32[11,128,2,512]{3,2,1,0:T(2,128)}, u32[]{:S(2)}, u32[]{:S(2)}) %collective-permute-start.2) | collective-permute-done | bytes 5767200 | tf_op jit(solution)/shard_map/ppermute | solution.py:23
  352.3 9.0 %fusion.76 = (f32[1408,1,512]{2,1,0:T(1,128)S(1)}, f32[1408,1,512]{2,1,0:T(1,128)S(1)}) fusion(f32[1408,2,512]{2,1,0:T(2,128)} %bitcast.19), kind=kLoop, calls=%fused_computation.93 | loop fusion | bytes 11534336 | tf_op jit(solution)/shard_map/slice | solution.py:85
  361.3 113.6 %collective-permute-done.3 = f32[11,128,2,512]{3,2,1,0:T(2,128)} collective-permute-done((f32[11,128,2,512]{3,2,1,0:T(2,128)}, f32[11,128,2,512]{3,2,1,0:T(2,128)}, u32[]{:S(2)}, u32[]{:S(2)}) %collective-permute-start.3) | collective-permute-done | bytes 5767200 | tf_op jit(solution)/shard_map/ppermute | solution.py:23
  474.9 10.6 %fusion.74 = (f32[1408,1,512]{2,1,0:T(1,128)}, f32[1408,1,512]{2,1,0:T(1,128)}) fusion(f32[1408,2,512]{2,1,0:T(2,128)} %bitcast.25), kind=kLoop, calls=%fused_computation.91 | loop fusion | bytes 11534336 | tf_op jit(solution)/shard_map/slice | solution.py:91
  485.6 2.8 fusion.27
  488.4 1.0 copy.111
  489.4 5.5 fusion.33
  494.9 4.0 fusion.3
  498.8 3.7 fusion.70
  502.6 2.8 convolution_subtract_fusion.1
  505.4 2.9 convolution_add_fusion
  508.3 3.3 fusion.13
  511.6 7.1 %fusion.12 = f32[1408,512]{0,1:T(8,128)} fusion(f32[512,1408]{1,0:T(8,128)S(1)} %fusion.33, f32[1408,1,512]{2,1,0:T(1,128)S(1)} %get-tuple-element.13, f32[1024,1024]{0,1:T(8,128)S(1)} %bitcast.133, s32[]{:T(128)S(6)} %select_n.52, s32[]{:T(128)S(6)} %select_n.56), kind=kOutput, calls=%fused_computation.19 | convolution fusion | flops 2215313408 | bytes 9699336 | tf_op jit(solution)/shard_map/dot_general | solution.py:14
  518.7 4.4 fusion.72
  523.2 5.1 fusion.16
  528.4 7.1 %fusion.22 = f32[1024,1408]{1,0:T(8,128)S(1)} fusion(f32[1408,1,512]{2,1,0:T(1,128)S(1)} %copy-done.11, f32[1024,1024]{1,0:T(8,128)} %copy-done.9, s32[]{:T(128)S(6)} %select_n.53), kind=kOutput, calls=%fused_computation.29 | convolution fusion | flops 4429185024 | bytes 10747908 | tf_op jit(solution)/shard_map/dot_general | solution.py:14
  535.5 7.3 %fusion.19 = f32[1024,1408]{1,0:T(8,128)} fusion(f32[1408,1,512]{2,1,0:T(1,128)S(1)} %copy-done.10, f32[1024,1024]{1,0:T(8,128)S(1)} %get-tuple-element.5, s32[]{:T(128)S(6)} %select_n.53), kind=kOutput, calls=%fused_computation.26 | convolution fusion | flops 4429185024 | bytes 10747908 | tf_op jit(solution)/shard_map/dot_general | solution.py:14
  542.8 13.3 %fusion.2 = f32[1408,1024]{0,1:T(8,128)} fusion(f32[1408,512]{0,1:T(8,128)S(1)} %fusion.13, f32[1408,512]{0,1:T(8,128)} %fusion.12, f32[1024,1408]{1,0:T(8,128)S(1)} %fusion.16, f32[1024,1408]{1,0:T(8,128)} %fusion.19, f32[1024,1408]{1,0:T(8,128)S(1)} %fusion.22, f32[1408,1,512]{2,1,0:T(1,128)} %get-tuple-element.9, f32[1024,1024]{1,0:T(8,128)} %copy-done.8, ...), kind=kOutput, calls=%fused_computation.4 | convolution fusion | flops 4436393984 | bytes 33816580 | tf_op jit(solution)/shard_map/dot_general | solution.py:14
  556.1 1.1 dynamic-slice_bitcast_fusion
  557.2 5.8 pad_maximum_fusion
  563.0 6.6 %copy.28 = f32[1536,1024]{1,0:T(8,128)} copy(f32[1536,1024]{0,1:T(8,128)} %pad_maximum_fusion) | data formatting | bytes 12582912 | tf_op jit(solution)/shard_map/concatenate | solution.py:93
  569.6 9.1 %reshape.52 = f32[12,128,2,512]{3,2,1,0:T(2,128)} reshape(f32[1536,1024]{1,0:T(8,128)} %copy.28) | data formatting | bytes 12582912 | tf_op jit(solution)/shard_map/reshape | solution.py:94
  (38 shorter events, 0.2 us)
Async XLA Ops:
  6.5 14.8 %slice-start = ((f32[12,128,2,512]{3,2,1,0:T(2,128)}), f32[1,128,2,512]{3,2,1,0:T(2,128)S(1)}, s32[]{:S(2)}) async-start(f32[12,128,2,512]{3,2,1,0:T(2,128)} %param.2), calls=%async_computation.4 | async-start | bytes 1048576 | tf_op jit(solution)/shard_map/slice | solution.py:55
  6.5 74.9 %all-gather.10.cloned.1.call-start = ((), (), s32[]{:S(2)}) async-start(), calls=%async_computation.3 | async-start | bytes 4325376 | tf_op jit(solution)/shard_map/all_gather | solution.py:51
  8.0 11.6 %collective-permute-start.1 = (f32[64,512]{1,0:T(8,128)S(1)}, f32[64,512]{1,0:T(8,128)S(1)}, u32[]{:S(2)}, u32[]{:S(2)}) collective-permute-start(f32[64,512]{1,0:T(8,128)S(1)} %bitcast.142), channel_id=1, source_target_pairs={{8,0},{9,1},{10,2},{11,3},{12,4},{13,5},{14,6},{15,7},{24,16},{25,... | collective-permute-start | bytes 393224 | tf_op jit(solution)/shard_map/ppermute | solution.py:49
  20.3 140.2 %all-gather.8.cloned.1.call-start = ((), (), s32[]{:S(2)}) async-start(), calls=%async_computation.2 | async-start | bytes 8650752 | tf_op jit(solution)/shard_map/all_gather | solution.py:44
  21.2 497.5 %all-gather.6.cloned.1.call-start = ((), (), s32[]{:S(2)}) async-start(), calls=%async_computation.1 | async-start | bytes 8912896 | tf_op jit(solution)/shard_map/all_gather | solution.py:74
  21.4 14.3 %collective-permute-start = (f32[128,2,512]{2,0,1:T(8,128)S(1)}, f32[128,2,512]{2,0,1:T(8,128)S(1)}, u32[]{:S(2)}, u32[]{:S(2)}) collective-permute-start(f32[128,2,512]{2,0,1:T(8,128)S(1)} %bitcast.137), channel_id=1, source_target_pairs={{16,0},{0,16},{17,1},{1,17},{18,2},{2,18},{19,3},{3,19},{20,4},{4,... | collective-permute-start | bytes 1572872 | tf_op jit(solution)/shard_map/ppermute | solution.py:23
  182.6 2.1 copy-start
  182.6 3.3 copy-start.2
  185.9 2.2 copy-start.5
  208.0 4.2 copy-start.3
  212.2 2.2 copy-start.6
  216.6 8.9 %slice-start.1 = ((s8[6291456]{0:T(1024)(128)(4,1)}), s8[2097152]{0:T(1024)(128)(4,1)S(1)}, s32[]{:S(2)}) async-start(s8[6291456]{0:T(1024)(128)(4,1)} %bitcast.134), calls=%async_computation.5 | async-start | bytes 4194304
  217.4 8.0 %slice-start.2 = ((s8[6291456]{0:T(1024)(128)(4,1)}), s8[4194304]{0:T(1024)(128)(4,1)S(1)}, s32[]{:S(2)}) async-start(s8[6291456]{0:T(1024)(128)(4,1)} %bitcast.134), calls=%async_computation.6 | async-start | bytes 8388608
  224.8 127.5 %collective-permute-start.2 = (f32[11,128,2,512]{3,2,1,0:T(2,128)}, f32[11,128,2,512]{3,2,1,0:T(2,128)}, u32[]{:S(2)}, u32[]{:S(2)}) collective-permute-start(f32[11,128,2,512]{3,2,1,0:T(2,128)} %slice.103), channel_id=1, source_target_pairs={{16,0},{0,16},{17,1},{1,17},{18,2},{2,18},{19,3},{3,19},{20,4},{4,... | collective-permute-start | bytes 17301512 | tf_op jit(solution)/shard_map/ppermute | solution.py:23
  229.9 245.0 %collective-permute-start.3 = (f32[11,128,2,512]{3,2,1,0:T(2,128)}, f32[11,128,2,512]{3,2,1,0:T(2,128)}, u32[]{:S(2)}, u32[]{:S(2)}) collective-permute-start(f32[11,128,2,512]{3,2,1,0:T(2,128)} %slice.109), channel_id=1, source_target_pairs={{16,0},{0,16},{17,1},{1,17},{18,2},{2,18},{19,3},{3,19},{20,4},{4,... | collective-permute-start | bytes 17301512 | tf_op jit(solution)/shard_map/ppermute | solution.py:23
  474.9 10.6 %copy-start.7 = (f32[128,8,2,512]{3,1,2,0:T(8,128)S(1)}, f32[128,8,2,512]{3,1,2,0:T(8,128)}, u32[]{:S(2)}) copy-start(f32[128,8,2,512]{3,1,2,0:T(8,128)} %copy.44) | copy-start | bytes 12582916
  485.6 2.8 copy-start.1
  489.4 5.5 copy-start.4
  518.7 4.5 copy-start.12
  523.2 5.2 copy-start.9
  523.2 12.3 %copy-start.8 = (f32[1024,1024]{1,0:T(8,128)}, f32[1024,1024]{1,0:T(8,128)S(1)}, u32[]{:S(2)}) copy-start(f32[1024,1024]{1,0:T(8,128)S(1)} %get-tuple-element.5) | copy-start | bytes 12582916
  523.2 5.2 copy-start.11
  528.4 7.1 %copy-start.10 = (f32[1408,1,512]{2,1,0:T(1,128)S(1)}, f32[1408,1,512]{2,1,0:T(1,128)}, u32[]{:S(2)}) copy-start(f32[1408,1,512]{2,1,0:T(1,128)} %get-tuple-element.12) | copy-start | bytes 8650756
Sparse Core Ops, SparseCore 0:
  20.4 60.9 all-gather.9
  84.5 75.9 all-gather.7
  217.6 73.4 all-gather.5
